TPU v7x, 256 devices: a whole 4x4x8 slice. The times are simulated.
256 devices in a mesh: slab: 2 (over core), grp: 16 (over y, x), col: 8 (over z).
Axes of the slice: x: 4, y: 4, z: 8, core: 2. Of those that a mesh axis runs over, the one named last changes fastest.
Arguments:
- fine_blocks: bfloat16 [2048, 27, 64, 64], P(('slab', 'grp', 'col')), may hold values from -4 to 4
- prolong: bfloat16 [2048, 64, 64], P(('slab', 'grp', 'col')), may hold values from -2 to 2
- column_ids: int32 [2048, 27], P(('slab', 'grp', 'col')), may hold values from 0 to 159
- aggregate_ids: int32 [2048], P(('slab', 'grp', 'col')), may hold values from 0 to 15, as said below
- live_rows: int32 [256], P(('slab', 'grp', 'col')), may hold values from 1 to 8, 1536 in all
Outputs:
- coarse: float32 [256, 80, 64, 64], P(('slab', 'grp', 'col'))
Inputs may be any that keep to these rules, and one draw needn't show every extreme that they name: `aggregate_ids`: among the 8 rows of one device no aggregate is named by more than 2 rows, and one aggregate is named by exactly 2 rows.
All inputs are finite; a program needn't handle non-finite values. No bound on the sum of `live_rows` on one device may be relied on, other than what follows from the above.
Results may differ from a plain program's by a relative error of at most 0.00035.
Values may be sent and summed in bfloat16 or wider, within the bound.
A program may use at most 256 MiB of HBM per device.

v0:
```python
import jax
import jax.numpy as jnp
from jax import lax
from jax.sharding import PartitionSpec as P


def extended(cells, sides, width):
    for axis, dim in sides:
        count = lax.axis_size(axis)
        ends = count - 1
        head = lax.slice_in_dim(cells, 0, width, axis=dim)
        tail = lax.slice_in_dim(cells, cells.shape[dim] - width, cells.shape[dim], axis=dim)
        cells = jnp.concatenate(
            [
                lax.ppermute(tail, axis, [(i, (i + 1) % count) for i in range(ends)]),
                cells,
                lax.ppermute(head, axis, [((i + 1) % count, i) for i in range(ends)]),
            ],
            axis=dim,
        )
    return cells


def per_device(fine_blocks, prolong, column_ids, aggregate_ids, live_rows):
    rows = prolong.shape[0]
    size = prolong.shape[1]
    groups = lax.axis_size("grp")
    width = 5 * groups
    split = groups * rows
    live_mask = (jnp.arange(rows, dtype=jnp.int32) < live_rows[0]).astype(jnp.bfloat16)
    masked = prolong * live_mask[:, None, None]
    group_tiles, group_aggs = (
        lax.all_gather(masked, "grp", axis=0, tiled=True),
        lax.all_gather(aggregate_ids, "grp", axis=0, tiled=True),
    )
    near_tiles, near_aggs = (
        extended(masked[None, None], (("slab", 0), ("col", 1)), 1),
        extended(aggregate_ids[None, None], (("slab", 0), ("col", 1)), 1),
    )
    side_tiles = jnp.concatenate(
        [near_tiles[0, 1], near_tiles[2, 1], near_tiles[1, 0], near_tiles[1, 2]], 0
    )
    side_aggs = jnp.concatenate(
        [near_aggs[0, 1], near_aggs[2, 1], near_aggs[1, 0], near_aggs[1, 2]], 0
    )
    tile_table = jnp.concatenate([group_tiles, side_tiles], 0)
    agg_table = jnp.concatenate([group_aggs, side_aggs], 0)
    direction_slot = jnp.where(column_ids < split, 0, 1 + (column_ids - split) // rows) * groups
    slot = (direction_slot + agg_table[column_ids]).astype(jnp.int32)
    picked = tile_table[column_ids]
    products = jnp.einsum(
        "rkab,rkbc->rkac", fine_blocks, picked, preferred_element_type=jnp.float32
    )
    triple = jnp.einsum(
        "rba,rkbc->rkac", masked.astype(jnp.float32), products, precision=lax.Precision.HIGHEST
    )
    keys = aggregate_ids[:, None] * width + slot
    partial_value = jax.ops.segment_sum(
        triple.reshape(-1, size, size), keys.reshape(-1), num_segments=groups * width
    )
    partial_value = partial_value.reshape(groups, width, size, size)
    return lax.psum_scatter(partial_value, "grp", scatter_dimension=0, tiled=True)


def solution(mesh):
    placed = (
        P(("slab", "grp", "col"), None, None, None),
        P(("slab", "grp", "col"), None, None),
        P(("slab", "grp", "col"), None),
        P(("slab", "grp", "col")),
        P(("slab", "grp", "col")),
    )
    return jax.shard_map(
        per_device,
        mesh=mesh,
        in_specs=placed,
        out_specs=P(("slab", "grp", "col"), None, None, None),
        check_vma=False,
    )
```

profile of v0, /device:TPU:96, one launch (start us, length us, event | category | flops | bytes accessed | tf_op | source)
XLA Modules:
  0.0 393.0 jit_solution(9922760944241048602)
XLA Ops:
  7.4 1.8 broadcast_multiply_fusion
  9.2 0.0 all-gather.2.cloned.1.call-update
  9.2 0.0 reduce-scatter.4.cloned.1.call-start
  9.2 1.3 collective-permute-start.1
  10.5 4.1 %collective-permute-start = (s32[1,1,8]{2,1,0:T(1,128)}, s32[1,1,8]{2,1,0:T(1,128)}, u32[]{:S(2)}, u32[]{:S(2)}) collective-permute-start(s32[1,1,8]{2,1,0:T(1,128)} %bitcast.44), channel_id=1, source_target_pairs={{0,128},{1,129},{2,130},{3,131},{4,132},{5,133},{6,134},{7,135},{8... | collective-permute-start | bytes 104 | tf_op jit(solution)/shard_map/ppermute | solution.py:15
  14.7 1.6 fusion.15
  16.3 1.3 collective-permute-start.5
  17.6 4.3 %collective-permute-start.4 = (bf16[1,1,8,64,64]{4,3,2,1,0:T(8,128)(2,1)}, bf16[1,1,8,64,64]{4,3,2,1,0:T(8,128)(2,1)}, u32[]{:S(2)}, u32[]{:S(2)}) collective-permute-start(bf16[1,1,8,64,64]{4,3,2,1,0:T(8,128)(2,1)} %fusion.15), channel_id=1, source_target_pairs={{0,128},{1,129},{2,130},{3,131},{4,132},{5,133},{6,134},{7,135},{8... | collective-permute-start | bytes 196616 | tf_op jit(solution)/shard_map/ppermute | solution.py:15
  21.9 0.7 compare_select_fusion
  22.6 0.1 reshape.17
  22.7 1.3 dynamic-slice
  24.6 0.9 dynamic-update-slice
  25.5 17.0 %all-reduce = s32[128]{0:T(128)} all-reduce(s32[128]{0:T(128)S(1)} %dynamic-update-slice), channel_id=1, replica_groups=mesh['slab'=2,'grp'=16,'col'=8] {'grp'}, use_global_device_ids=true, to_apply=%add | all-reduce | flops 128 | bytes 1024
  42.5 1.2 broadcast_multiply_fusion.1
  43.7 0.0 collective-permute-done.1
  43.7 0.0 collective-permute-done
  43.7 0.7 pad_add_fusion
  44.5 2.0 collective-permute-start.3
  46.5 5.0 %collective-permute-start.2 = (s32[3,1,8]{2,1,0:T(1,128)S(1)}, s32[3,1,8]{2,1,0:T(1,128)S(1)}, u32[]{:S(2)}, u32[]{:S(2)}) collective-permute-start(s32[3,1,8]{2,1,0:T(1,128)S(1)} %pad_add_fusion), channel_id=1, source_target_pairs={{0,1},{1,2},{2,3},{3,4},{4,5},{5,6},{6,7},{8,9},{9,10},{10,11},{11... | collective-permute-start | bytes 296 | tf_op jit(solution)/shard_map/ppermute | solution.py:15
  51.5 0.5 slice_bitcast_fusion.2
  52.0 0.8 collective-permute-done.2
  52.8 0.8 concatenate.13
  53.6 1.9 gather_fusion
  55.5 0.1 reshape.16
  55.6 0.7 fusion.10
  56.3 0.1 reshape.33
  56.4 0.0 collective-permute-done.5
  56.4 0.0 collective-permute-done.4
  56.4 1.9 pad_maximum_fusion
  58.3 1.9 collective-permute-start.7
  60.3 5.4 %collective-permute-start.6 = (bf16[3,1,8,64,64]{4,3,2,1,0:T(8,128)(2,1)}, bf16[3,1,8,64,64]{4,3,2,1,0:T(8,128)(2,1)}, u32[]{:S(2)}, u32[]{:S(2)}) collective-permute-start(bf16[3,1,8,64,64]{4,3,2,1,0:T(8,128)(2,1)} %pad_maximum_fusion), channel_id=1, source_target_pairs={{0,1},{1,2},{2,3},{3,4},{4,5},{5,6},{6,7},{8,9},{9,10},{10,11},{11... | collective-permute-start | bytes 589832 | tf_op jit(solution)/shard_map/ppermute | solution.py:15
  65.7 0.0 all-gather.2.cloned.1.call-done
  65.7 3.1 constant_dynamic-update-slice_fusion
  68.8 1.6 bitcast_dynamic-update-slice_fusion.1
  70.4 1.6 bitcast_dynamic-update-slice_fusion
  71.9 0.0 collective-permute-done.6
  71.9 1.6 fusion.3
  73.5 1.6 fusion.2
  75.1 4.6 %gather_fusion.1 = bf16[216,64,64]{2,1,0:T(8,128)(2,1)} fusion(bf16[160,64,64]{2,1,0:T(8,128)(2,1)} %fusion.2, s32[1024]{0:T(1024)S(1)} %pad_clamp_fusion), kind=kCustom, calls=%fused_computation.1 | custom fusion | bytes 3539808 | tf_op jit(solution)/shard_map/gather | solution.py:50
  79.6 4.0 %fusion.12 = f32[8,27,64,64]{3,2,1,0:T(8,128)S(1)} fusion(bf16[8,27,64,64]{3,2,1,0:T(8,128)(2,1)} %bitcast.42, bf16[8,27,64,64]{3,2,1,0:T(8,128)(2,1)S(1)} %copy-done), kind=kOutput, calls=%fused_computation.34 | convolution fusion | flops 113246208 | bytes 7077888 | tf_op jit(solution)/shard_map/rkab,rkbc->rkac/dot_general | solution.py:51
  83.7 5.4 %fusion = f32[8,27,64,64]{3,2,1,0:T(8,128)} fusion(f32[8,27,64,64]{3,2,1,0:T(8,128)S(1)} %fusion.12, bf16[8,64,64]{2,1,0:T(8,128)(2,1)S(1)} %copy-done.2), kind=kOutput, calls=%fused_computation.3 | convolution fusion | flops 679477248 | bytes 7143424 | tf_op jit(solution)/shard_map/rba,rkbc->rkac/dot_general | solution.py:54
  89.1 8.4 %copy.10 = f32[216,64,64]{2,1,0:T(8,128)} copy(f32[216,64,64]{1,2,0:T(8,128)} %bitcast.41) | data formatting | bytes 7077888 | tf_op jit(solution)/shard_map/reshape | solution.py:59
  97.6 13.7 %broadcast_in_dim.19 = f32[1280,64,64]{2,1,0:T(8,128)} broadcast(f32[]{:T(128)} %constant.9.clone.1), dimensions={} | broadcast | bytes 20971524 | tf_op jit(solution)/shard_map/broadcast_in_dim | solution.py:58
  111.3 34.5 %scatter_fusion = f32[1280,64,64]{2,1,0:T(8,128)} fusion(f32[1280,64,64]{2,1,0:T(8,128)} %broadcast_in_dim.19, s32[216]{0:T(256)S(1)} %reshape.33, f32[216,64,64]{2,1,0:T(8,128)} %copy.10), kind=kCustom, calls=%fused_computation.2 | custom fusion | flops 884736 | bytes 10617696 | tf_op jit(solution)/shard_map/scatter-add | solution.py:58
  145.8 42.5 %copy.12 = f32[16,80,64,64]{1,3,2,0:T(8,128)} copy(f32[16,80,64,64]{3,2,1,0:T(8,128)} %bitcast.40) | data formatting | bytes 41943040 | tf_op jit(solution)/shard_map/reshape | solution.py:61
  188.4 0.0 reduce-scatter.4.cloned.1.call-update
  188.4 0.0 copy-start.1
  188.4 197.7 %reduce-scatter.4.cloned.1.call-done = f32[1,80,64,64]{1,3,2,0:T(8,128)} async-done(((f32[16,80,64,64]{1,3,2,0:T(8,128)}), f32[1,80,64,64]{1,3,2,0:T(8,128)}) %reduce-scatter.4.cloned.1.call-update) | async-done | bytes 1310736
  (14 shorter events, 0.0 us)
Async XLA Ops:
  6.5 73.1 %copy-start = (bf16[8,27,64,64]{3,2,1,0:T(8,128)(2,1)S(1)}, bf16[8,27,64,64]{3,2,1,0:T(8,128)(2,1)}, u32[]{:S(2)}) copy-start(bf16[8,27,64,64]{3,2,1,0:T(8,128)(2,1)} %param.5) | copy-start | bytes 5308420
  6.5 49.1 %copy-start.3 = (s32[8,27]{1,0:T(8,128)S(1)}, s32[8,27]{1,0:T(8,128)}, u32[]{:S(2)}) copy-start(s32[8,27]{1,0:T(8,128)} %param.7) | copy-start | bytes 2596
  6.5 59.1 %all-gather.2.cloned.1.call-start = ((), (), s32[]{:S(2)}) async-start(), calls=%async_computation.1 | async-start | bytes 2228224 | tf_op jit(solution)/shard_map/all_gather | solution.py:33
  9.2 376.9 %reduce-scatter.4.cloned.1.call-start = ((), (), s32[]{:S(2)}) async-start(), calls=%async_computation.2 | async-start | bytes 35651584
  9.2 34.5 %collective-permute-start.1 = (s32[1,1,8]{2,1,0:T(1,128)}, s32[1,1,8]{2,1,0:T(1,128)}, u32[]{:S(2)}, u32[]{:S(2)}) collective-permute-start(s32[1,1,8]{2,1,0:T(1,128)} %bitcast.43), channel_id=1, source_target_pairs={{128,0},{129,1},{130,2},{131,3},{132,4},{133,5},{134,6},{135,7},{1... | collective-permute-start | bytes 104 | tf_op jit(solution)/shard_map/ppermute | solution.py:17
  10.5 33.2 %collective-permute-start = (s32[1,1,8]{2,1,0:T(1,128)}, s32[1,1,8]{2,1,0:T(1,128)}, u32[]{:S(2)}, u32[]{:S(2)}) collective-permute-start(s32[1,1,8]{2,1,0:T(1,128)} %bitcast.44), channel_id=1, source_target_pairs={{0,128},{1,129},{2,130},{3,131},{4,132},{5,133},{6,134},{7,135},{8... | collective-permute-start | bytes 104 | tf_op jit(solution)/shard_map/ppermute | solution.py:15
  16.3 40.1 %collective-permute-start.5 = (bf16[1,1,8,64,64]{4,3,2,1,0:T(8,128)(2,1)}, bf16[1,1,8,64,64]{4,3,2,1,0:T(8,128)(2,1)}, u32[]{:S(2)}, u32[]{:S(2)}) collective-permute-start(bf16[1,1,8,64,64]{4,3,2,1,0:T(8,128)(2,1)} %fusion.15), channel_id=1, source_target_pairs={{128,0},{129,1},{130,2},{131,3},{132,4},{133,5},{134,6},{135,7},{1... | collective-permute-start | bytes 196616 | tf_op jit(solution)/shard_map/ppermute | solution.py:17
  17.6 38.9 %collective-permute-start.4 = (bf16[1,1,8,64,64]{4,3,2,1,0:T(8,128)(2,1)}, bf16[1,1,8,64,64]{4,3,2,1,0:T(8,128)(2,1)}, u32[]{:S(2)}, u32[]{:S(2)}) collective-permute-start(bf16[1,1,8,64,64]{4,3,2,1,0:T(8,128)(2,1)} %fusion.15), channel_id=1, source_target_pairs={{0,128},{1,129},{2,130},{3,131},{4,132},{5,133},{6,134},{7,135},{8... | collective-permute-start | bytes 196616 | tf_op jit(solution)/shard_map/ppermute | solution.py:15
  44.5 7.1 %collective-permute-start.3 = (s32[3,1,8]{2,1,0:T(1,128)S(1)}, s32[3,1,8]{2,1,0:T(1,128)S(1)}, u32[]{:S(2)}, u32[]{:S(2)}) collective-permute-start(s32[3,1,8]{2,1,0:T(1,128)S(1)} %pad_add_fusion), channel_id=1, source_target_pairs={{1,0},{2,1},{3,2},{4,3},{5,4},{6,5},{7,6},{9,8},{10,9},{11,10},{12... | collective-permute-start | bytes 296 | tf_op jit(solution)/shard_map/ppermute | solution.py:17
  46.5 6.3 %collective-permute-start.2 = (s32[3,1,8]{2,1,0:T(1,128)S(1)}, s32[3,1,8]{2,1,0:T(1,128)S(1)}, u32[]{:S(2)}, u32[]{:S(2)}) collective-permute-start(s32[3,1,8]{2,1,0:T(1,128)S(1)} %pad_add_fusion), channel_id=1, source_target_pairs={{0,1},{1,2},{2,3},{3,4},{4,5},{5,6},{6,7},{8,9},{9,10},{10,11},{11... | collective-permute-start | bytes 296 | tf_op jit(solution)/shard_map/ppermute | solution.py:15
  58.3 15.2 %collective-permute-start.7 = (bf16[3,1,8,64,64]{4,3,2,1,0:T(8,128)(2,1)}, bf16[3,1,8,64,64]{4,3,2,1,0:T(8,128)(2,1)}, u32[]{:S(2)}, u32[]{:S(2)}) collective-permute-start(bf16[3,1,8,64,64]{4,3,2,1,0:T(8,128)(2,1)} %pad_maximum_fusion), channel_id=1, source_target_pairs={{1,0},{2,1},{3,2},{4,3},{5,4},{6,5},{7,6},{9,8},{10,9},{11,10},{12... | collective-permute-start | bytes 589832 | tf_op jit(solution)/shard_map/ppermute | solution.py:17
  60.3 11.7 %collective-permute-start.6 = (bf16[3,1,8,64,64]{4,3,2,1,0:T(8,128)(2,1)}, bf16[3,1,8,64,64]{4,3,2,1,0:T(8,128)(2,1)}, u32[]{:S(2)}, u32[]{:S(2)}) collective-permute-start(bf16[3,1,8,64,64]{4,3,2,1,0:T(8,128)(2,1)} %pad_maximum_fusion), channel_id=1, source_target_pairs={{0,1},{1,2},{2,3},{3,4},{4,5},{5,6},{6,7},{8,9},{9,10},{10,11},{11... | collective-permute-start | bytes 589832 | tf_op jit(solution)/shard_map/ppermute | solution.py:15
  79.6 4.0 %copy-start.2 = (bf16[8,64,64]{2,1,0:T(8,128)(2,1)S(1)}, bf16[8,64,64]{2,1,0:T(8,128)(2,1)}, u32[]{:S(2)}) copy-start(bf16[8,64,64]{2,1,0:T(8,128)(2,1)} %broadcast_multiply_fusion) | copy-start | bytes 196612
  188.4 197.8 %copy-start.1 = (bf16[8,27,64,64]{3,2,1,0:T(8,128)(2,1)S(1)}, bf16[8,27,64,64]{3,2,1,0:T(8,128)(2,1)}, u32[]{:S(2)}) copy-start(bf16[8,27,64,64]{3,2,1,0:T(8,128)(2,1)} %param.5) | copy-start | bytes 5308420
Sparse Core Ops, SparseCore 0:
  9.8 51.8 all-gather.1
  188.5 197.5 reduce-scatter.3
where the time goes:
time: 397 us; the launch traced here: 393 us
  waiting for transfers between devices  199 us (50%)
  local copies, waits for them, and re-layouts  84.2 us (21%)
  other arithmetic  43.2 us (11%)
  starting transfers between devices  25.4 us (6%)
  blocking collectives  17 us (4%)
  between operations  15 us (4%)
  matrix products  9.49 us (2%)
    unnamed x3, waiting for transfers between devices  198 us
    reshape x1, local copies, waits for them, and re-layouts, per_device(): partial_value = partial_value.reshape(groups, width, size, size)  42.5 us
    scatter-add x1, other arithmetic, per_device(): jax.ops.segment_sum(triple.reshape(-1, size, size), keys.reshape(-1), num...  34.5 us
    ppermute x4, starting transfers between devices, extended(): lax.ppermute(tail, axis, [(i, (i + 1) % count) for i in range(ends)])  18.8 us
    unnamed x1, blocking collectives  17 us
    broadcast_in_dim x1, local copies, waits for them, and re-layouts, per_device(): jax.ops.segment_sum(triple.reshape(-1, size, size), keys.reshape(-1), num...  13.7 us
    unnamed x15, local copies, waits for them, and re-layouts  9.95 us
    reshape x1, local copies, waits for them, and re-layouts, per_device(): triple.reshape(-1, size, size)  8.44 us
  transfers between devices with their start and end apart: 10, of which 2 were waited for; matrix products, arithmetic and copies ran while one was open for 5% of the time, Pallas kernels for 0%

commit v1 on v0

v1 whole, which is shorter than its diff:
```python
import functools

import jax
import jax.numpy as jnp
from jax import lax
from jax.experimental import pallas as pl
from jax.experimental.pallas import tpu as pltpu
from jax.sharding import PartitionSpec as P

MESH = pl.DeviceIdType.MESH
GRP, SIDE, NCOL = 16, 4, 8
RB, KA, B = 8, 27, 64
KP = 28
CHUNKS, PER = 2, 4
CR = KP * PER
WIDTH = 80
TILES = 160
MSG = 272
HALF = (pl.ds(0, 144), pl.ds(144, 128))
FULL = 32760.0
F32, BF16 = jnp.float32, jnp.bfloat16


def code(x, inverse):
    v = jnp.sqrt(jnp.abs(x) * inverse) + 0.5
    return jnp.where(x < 0, -v, v).astype(jnp.int32).astype(jnp.int16)


def remote(src, dst, send, recv, where):
    return pltpu.make_async_remote_copy(
        src_ref=src, dst_ref=dst, send_sem=send, recv_sem=recv, device_id=where, device_id_type=MESH
    )


def kernel(
    blocks_hbm, prolong, ids_vec, ids, aggs, live,
    result,
    blocks, tiles, table, flipped, u, ids_row, stage, out1, got1, side_out, side, total, out2, scale_out, got2, scale2,
    block_sem, ag_send, ag_recv, near_send, near_recv,
    d_send, d_recv, s_send, s_recv, e_send, e_recv, f_send, f_recv,
):
    s, g, c = lax.axis_index("slab"), lax.axis_index("grp"), lax.axis_index("col")
    gy, gx = g // SIDE, lax.rem(g, SIDE)
    bar = pltpu.get_barrier_semaphore()
    for p in range(1, GRP):
        pl.semaphore_signal(bar, inc=1, device_id={"grp": lax.rem(g + p, GRP)}, device_id_type=MESH)
    pl.semaphore_signal(bar, inc=1, device_id={"slab": 1 - s}, device_id_type=MESH)

    @pl.when(c > 0)
    def _():
        pl.semaphore_signal(bar, inc=1, device_id={"col": c - 1}, device_id_type=MESH)

    @pl.when(c < NCOL - 1)
    def _():
        pl.semaphore_signal(bar, inc=1, device_id={"col": c + 1}, device_id_type=MESH)

    block_copy = pltpu.make_async_copy(blocks_hbm, blocks, block_sem)
    block_copy.start()

    alive = jnp.full((B, B), live[0], jnp.int32)
    for r in range(0, RB, 2):
        left, right = (
            jnp.where(alive > r + d, prolong[r + d].astype(F32), 0.0) for d in range(2)
        )
        tiles[g, 32 * r : 32 * r + B, :] = jnp.concatenate([left, right], axis=1).astype(BF16)
        flipped[r] = left.T.astype(BF16)
        flipped[r + 1] = right.T.astype(BF16)
    sub16 = lax.broadcasted_iota(jnp.int32, (16, 128), 0)
    agg_rows = jnp.zeros((16, 128), F32)
    for r in range(RB):
        agg_rows = jnp.where(sub16 == r, aggs[r].astype(F32), agg_rows)
    tiles[g, 256:MSG, :] = agg_rows.astype(BF16)

    tiles[GRP + s] = jnp.zeros((MSG, 128), BF16)

    @pl.when(c == 0)
    def _():
        tiles[GRP + 2] = jnp.zeros((MSG, 128), BF16)

    @pl.when(c == NCOL - 1)
    def _():
        tiles[GRP + 3] = jnp.zeros((MSG, 128), BF16)

    cols = (c + NCOL - 1) // NCOL + (2 * NCOL - 2 - c) // NCOL
    pl.semaphore_wait(bar, GRP + cols)

    sends = []

    def spread(slot, half, y, x, source):
        copy = remote(
            tiles.at[slot, HALF[half]],
            tiles.at[slot, HALF[half]],
            ag_send.at[len(sends)],
            ag_recv.at[source * 2 + half],
            {"grp": y * SIDE + x},
        )
        copy.start()
        sends.append(copy)

    def arrived(dy, dx, half):
        slot = lax.rem(gy + dy, SIDE) * SIDE + lax.rem(gx + dx, SIDE)
        remote(
            tiles.at[slot, HALF[half]], tiles.at[slot, HALF[half]],
            ag_send.at[0], ag_recv.at[(dy * SIDE + dx) * 2 + half], {"grp": lax.rem(g + 1, GRP)},
        ).wait_recv()
        return slot

    for d in (1, 3, 2):
        back = SIDE - d
        spread(g, 0, gy, lax.rem(gx + d, SIDE), back)
        spread(g, 1, lax.rem(gy + d, SIDE), gx, back * SIDE)
    for d in (1, 3, 2):
        back = SIDE - d
        spread(g, 1, gy, lax.rem(gx + d, SIDE), back)
        spread(g, 0, lax.rem(gy + d, SIDE), gx, back * SIDE)

    def near(k, slot, where):
        return remote(tiles.at[g], tiles.at[slot], near_send.at[k], near_recv.at[k], where)

    near(0, GRP + s, {"slab": 1 - s}).start()

    @pl.when(c < NCOL - 1)
    def _():
        near(1, GRP + 2, {"col": c + 1}).start()

    @pl.when(c > 0)
    def _():
        near(2, GRP + 3, {"col": c - 1}).start()

    block_copy.wait()

    def u_row(i, carry):
        for k in range(0, KP, 2):
            left = jnp.dot(flipped[i], blocks[i, k], preferred_element_type=F32)
            if k + 1 < KA:
                right = jnp.dot(flipped[i], blocks[i, k + 1], preferred_element_type=F32)
            else:
                right = jnp.zeros((B, B), F32)
            value = jnp.concatenate([left, right], axis=1)
            high = value.astype(BF16)
            u[i, k // 2, 0:B, :] = high
            u[i, k // 2, B : 2 * B, :] = (value - high.astype(F32)).astype(BF16)
        return carry

    wide = lax.broadcasted_iota(jnp.int32, (B, 128), 1) < B

    def unfold(slot):
        def pair(n, carry):
            both = tiles[slot, pl.ds(pl.multiple_of(n * B, B), B), :].astype(F32)
            turned = pltpu.roll(both, B, 1)
            at = slot * RB + 2 * n
            table[at] = jnp.where(wide, both, 0.0).astype(BF16)
            table[at + 1] = jnp.where(wide, turned, 0.0).astype(BF16)
            table[TILES + at] = jnp.where(wide, 0.0, turned).astype(BF16)
            table[TILES + at + 1] = jnp.where(wide, 0.0, both).astype(BF16)
            return carry

        lax.fori_loop(0, RB // 2, pair, 0)

    lax.fori_loop(0, 2, u_row, 0)

    for e in (1, 3, 2):
        slot = arrived(0, e, 0)
        for d in (1, 3, 2):
            spread(slot, 0, lax.rem(gy + d, SIDE), gx, (SIDE - d) * SIDE + e)
        slot = arrived(e, 0, 1)
        for d in (1, 3, 2):
            spread(slot, 1, gy, lax.rem(gx + d, SIDE), e * SIDE + SIDE - d)

    lax.fori_loop(2, RB, u_row, 0)
    unfold(g)
    for e in (1, 3, 2):
        unfold(arrived(0, e, 1))
        unfold(arrived(e, 0, 0))
    near(0, GRP + 1 - s, {"slab": 1 - s}).wait_recv()

    @pl.when(c > 0)
    def _():
        near(1, GRP + 2, {"col": c - 1}).wait_recv()

    @pl.when(c < NCOL - 1)
    def _():
        near(2, GRP + 3, {"col": c + 1}).wait_recv()

    for slot in range(GRP, GRP + 4):
        unfold(slot)
    for e in (1, 3, 2):
        for f in (1, 3, 2):
            arrived(e, f, 0)
            unfold(arrived(e, f, 1))

    ids_row[...] = jnp.full((8, 128), -1, jnp.int32)
    ids_row[:, 0:KA] = ids_vec[...]
    lane = lax.broadcasted_iota(jnp.int32, (8, 128), 1)
    sub = lax.broadcasted_iota(jnp.int32, (8, 128), 0)
    for ch in range(CHUNKS):
        q = jnp.full((8, 128), -1, jnp.int32)
        owner = jnp.zeros((8, 128), F32)
        for ii in range(PER):
            i = PER * ch + ii
            row = jnp.broadcast_to(ids_row[i : i + 1, :], (8, 128))
            inside = (lane >= KP * ii) & (lane < KP * (ii + 1))
            q = jnp.where(inside, pltpu.roll(row, KP * ii, 1) if ii else row, q)
            owner = jnp.where(inside, aggs[i].astype(F32), owner)
        slot = jnp.zeros((8, 128), F32)
        for d in range(GRP + 4):
            base = 0 if d < GRP else (d - GRP + 1) * GRP
            named = tiles[d, 256:MSG, :].astype(F32)[0:8]
            slot = slot + jnp.where(q == sub + 8 * d, named + base, 0.0)
        slot = jnp.broadcast_to(jnp.sum(slot, axis=0, keepdims=True), (8, 128))
        key = jnp.where(q < 0, -1.0, owner * WIDTH + slot)
        side_out[ch] = jnp.where(sub == 0, key, 0.0)

    low = lax.broadcasted_iota(jnp.int32, (8, 128), 1) < B

    def piece(ch, p):
        where = lax.bitwise_xor(g, p)
        return (
            remote(out1.at[ch, where], got1.at[ch, g], d_send.at[ch, p], d_recv.at[ch, p], {"grp": where}),
            remote(side_out.at[ch], side.at[ch, g], s_send.at[ch, p], s_recv.at[ch, p], {"grp": where}),
        )

    for ch in range(CHUNKS):
        def t_row(ii, scales, ch=ch):
            i = PER * ch + ii
            top = jnp.zeros((8, 128), F32)
            for k in range(0, KP, 2):
                weights = jnp.concatenate(
                    [table[ids[i, k]], table[TILES + ids[i, min(k + 1, KA - 1)]]], axis=0
                )
                both = jnp.dot(u[i, k // 2], weights, preferred_element_type=F32)
                value = both[0:B] + both[B : 2 * B]
                top = jnp.maximum(top, jnp.max(jnp.abs(value).reshape(8, 8, 128), axis=0))
                for half in range(2):
                    for w in range(2):
                        first = value[32 * w + 8 * half : 32 * w + 8 * half + 8]
                        second = value[32 * w + 16 + 8 * half : 32 * w + 24 + 8 * half]
                        at = CR * (GRP * w + 8 * half) + KP * ii + k
                        stage[pl.ds(at, 8, stride=CR), :] = jnp.where(low, first, pltpu.roll(second, B, 1))
                        stage[pl.ds(at + 1, 8, stride=CR), :] = jnp.where(low, pltpu.roll(first, B, 1), second)
            most = jnp.max(jnp.max(top, axis=1, keepdims=True), axis=0, keepdims=True)
            most = jnp.broadcast_to(most, (8, 128))
            unit = (jnp.maximum(most, 1e-25) * (1.004 / (FULL * FULL))).astype(BF16).astype(F32)
            return tuple(jnp.where(ii == n, unit, scales[n]) for n in range(PER))

        scales = lax.fori_loop(0, PER, t_row, tuple(jnp.zeros((8, 128), F32) for _ in range(PER)))
        unit_row = jnp.zeros((8, 128), F32)
        row_of = lax.broadcasted_iota(jnp.int32, (CR, 128), 0)
        inverse = jnp.zeros((CR, 128), F32)
        for ii in range(PER):
            unit_row = jnp.where((lane >= KP * ii) & (lane < KP * (ii + 1)), scales[ii], unit_row)
            inverse = jnp.where(row_of >= KP * ii, (1.0 / scales[ii])[0:1], inverse)
        side_out[ch] = jnp.where(sub == 1, unit_row, side_out[ch])
        side[ch, g] = side_out[ch]

        def coded(where, ch=ch, inverse=inverse):
            first = code(stage[pl.ds(pl.multiple_of(where * CR, 16), CR), :], inverse)
            second = code(stage[pl.ds(pl.multiple_of((GRP + where) * CR, 16), CR), :], inverse)
            return jnp.concatenate([first, second], axis=1)

        got1[ch, g] = coded(g)

        def emit(p, carry, ch=ch):
            where = lax.bitwise_xor(g, p)
            out1[ch, where] = coded(where)
            data, extra = piece(ch, p)
            extra.start()
            data.start()
            return carry

        lax.fori_loop(1, GRP, emit, 0)

    total[...] = jnp.zeros_like(total)
    quarter = 4 * WIDTH

    def add(ch, source):
        info = side[ch, source]
        v = got1[ch, source].astype(F32)
        v = v * jnp.abs(v)
        high = v.astype(BF16)
        lower = (v - high.astype(F32)).astype(BF16)
        key = info[0:1, 0:CR]
        unit = info[1:2, 0:CR]
        for n in range(4):
            row = lax.broadcasted_iota(jnp.int32, (quarter, CR), 0).astype(F32) + float(n * quarter)
            pick = jnp.where(row == key, unit, 0.0).astype(BF16)
            total[n * quarter : (n + 1) * quarter, :] += jnp.dot(
                pick, high, preferred_element_type=F32
            ) + jnp.dot(pick, lower, preferred_element_type=F32)

    for ch in range(CHUNKS):
        add(ch, g)

        def take(p, carry, ch=ch):
            data, extra = piece(ch, p)
            extra.wait_recv()
            data.wait_recv()
            add(ch, lax.bitwise_xor(g, p))
            return carry

        lax.fori_loop(1, GRP, take, 0)

    def home(p):
        where = lax.bitwise_xor(g, p)
        return (
            remote(out2.at[where], got2.at[g], e_send.at[p], e_recv.at[p], {"grp": where}),
            remote(scale_out.at[where], scale2.at[g], f_send.at[p], f_recv.at[p], {"grp": where}),
        )

    def owned(where):
        value = total[pl.ds(pl.multiple_of(where * WIDTH, 16), WIDTH), :]
        most = jnp.max(jnp.max(jnp.abs(value), axis=1, keepdims=True), axis=0, keepdims=True)
        unit = jnp.maximum(most, 1e-25) * (1.004 / (FULL * FULL))
        return code(value, 1.0 / unit), jnp.broadcast_to(unit, (8, 128))

    got2[g], scale2[g] = owned(g)

    def give(p, carry):
        where = lax.bitwise_xor(g, p)
        out2[where], scale_out[where] = owned(where)
        data, extra = home(p)
        extra.start()
        data.start()
        return carry

    lax.fori_loop(1, GRP, give, 0)

    def place(m):
        v = got2[m].astype(F32)
        v = v * jnp.abs(v) * scale2[m][0:1, 0:1]
        for h in range(2):
            flat = v[:, 128 * h : 128 * h + 128].T
            result[2 * GRP * h + m] = flat[0:B]
            result[2 * GRP * h + GRP + m] = flat[B : 2 * B]

    place(g)

    def finish(p, carry):
        data, extra = home(p)
        extra.wait()
        data.wait()
        place(lax.bitwise_xor(g, p))
        for ch in range(CHUNKS):
            data, extra = piece(ch, p)
            extra.wait_send()
            data.wait_send()
        return carry

    lax.fori_loop(1, GRP, finish, 0)
    for copy in sends:
        copy.wait_send()
    near(0, GRP + s, {"slab": 1 - s}).wait_send()

    @pl.when(c < NCOL - 1)
    def _():
        near(1, GRP + 2, {"col": c + 1}).wait_send()

    @pl.when(c > 0)
    def _():
        near(2, GRP + 3, {"col": c - 1}).wait_send()


def per_device(fine_blocks, prolong, column_ids, aggregate_ids, live_rows):
    vmem = pl.BlockSpec(memory_space=pltpu.VMEM)
    smem = pl.BlockSpec(memory_space=pltpu.SMEM)
    dma = pltpu.SemaphoreType.DMA
    out = pl.pallas_call(
        kernel,
        out_shape=jax.ShapeDtypeStruct((B, B, WIDTH), F32),
        in_specs=[pl.BlockSpec(memory_space=pl.ANY), vmem, vmem, smem, smem, smem],
        out_specs=vmem,
        scratch_shapes=[
            pltpu.VMEM((RB, KA, B, B), BF16),
            pltpu.VMEM((GRP + 4, MSG, 128), BF16),
            pltpu.VMEM((2 * TILES, B, 128), BF16),
            pltpu.VMEM((RB, B, B), BF16),
            pltpu.VMEM((RB, KP // 2, 2 * B, 128), BF16),
            pltpu.VMEM((8, 128), jnp.int32),
            pltpu.VMEM((2 * GRP * CR, 128), F32),
            pltpu.VMEM((CHUNKS, GRP, CR, 256), jnp.int16),
            pltpu.VMEM((CHUNKS, GRP, CR, 256), jnp.int16),
            pltpu.VMEM((CHUNKS, 8, 128), F32),
            pltpu.VMEM((CHUNKS, GRP, 8, 128), F32),
            pltpu.VMEM((GRP * WIDTH, 256), F32),
            pltpu.VMEM((GRP, WIDTH, 256), jnp.int16),
            pltpu.VMEM((GRP, 8, 128), F32),
            pltpu.VMEM((GRP, WIDTH, 256), jnp.int16),
            pltpu.VMEM((GRP, 8, 128), F32),
            dma,
            dma((32,)),
            dma((32,)),
            dma((3,)),
            dma((3,)),
            dma((CHUNKS, GRP)),
            dma((CHUNKS, GRP)),
            dma((CHUNKS, GRP)),
            dma((CHUNKS, GRP)),
            dma((GRP,)),
            dma((GRP,)),
            dma((GRP,)),
            dma((GRP,)),
        ],
        compiler_params=pltpu.CompilerParams(
            collective_id=0, has_side_effects=True, vmem_limit_bytes=58 * 2**20
        ),
    )(fine_blocks, prolong, column_ids, column_ids, aggregate_ids, live_rows)
    return out.transpose(2, 0, 1)[None]


def solution(mesh):
    rows = ("slab", "grp", "col")
    return jax.shard_map(
        per_device,
        mesh=mesh,
        in_specs=(
            P(rows, None, None, None),
            P(rows, None, None),
            P(rows, None),
            P(rows),
            P(rows),
        ),
        out_specs=P(rows, None, None, None),
        check_vma=False,
    )
```

time: 397 us -> 70.1 us (0.18)
  waiting for transfers between devices: 199 us -> 0 us
  local copies, waits for them, and re-layouts: 84.2 us -> 3.16 us
  Pallas kernels: 0 us -> 66.2 us
  other arithmetic: 43.2 us -> 0 us
  starting transfers between devices: 25.4 us -> 0 us
  blocking collectives: 17 us -> 0 us
  between operations: 15 us -> 0.66 us
  matrix products: 9.49 us -> 0 us
    unnamed x3 -> x0, waiting for transfers between devices: 198 us -> none
    pallas_call x0 -> x1, Pallas kernels: none -> 66.2 us  [per_device(): pl.pallas_call(kernel, out_shape=jax.ShapeDtypeStruct((B, B, WIDTH), F32)...]
    reshape x2 -> x0, local copies, waits for them, and re-layouts: 51 us -> none  [the longest x1 42.5 us: per_device(): partial_value = partial_value.reshape(groups, width, size, size)]
    scatter-add x1 -> x0, other arithmetic: 34.5 us -> none  [per_device(): jax.ops.segment_sum(triple.reshape(-1, size, size), keys.reshape(-1), num...]
    ppermute x8 -> x0, starting transfers between devices: 25.3 us -> none  [the longest x4 18.8 us: extended(): lax.ppermute(tail, axis, [(i, (i + 1) % count) for i in range(ends)])]
    unnamed x1 -> x0, blocking collectives: 17 us -> none
    broadcast_in_dim x2 -> x0, local copies, waits for them, and re-layouts: 13.8 us -> none  [the longest x1 13.7 us: per_device(): jax.ops.segment_sum(triple.reshape(-1, size, size), keys.reshape(-1), num...]
    dot_general x2 -> x0, matrix products: 9.49 us -> none  [the longest x1 5.45 us: per_device(): jnp.einsum('rba,rkbc->rkac', masked.astype(jnp.float32), products, precis...]
  transfers between devices with their start and end apart: 10 -> 0, of which waited for: 2 -> 0; matrix products, arithmetic and copies ran while one was open for 5% -> 0% of each run, Pallas kernels for 0% -> 0%
where the time goes in v1:
time: 70.1 us; the launch traced here: 70 us
  Pallas kernels  66.2 us (94%)
  local copies, waits for them, and re-layouts  3.16 us (5%)
    pallas_call x1, Pallas kernels, per_device(): pl.pallas_call(kernel, out_shape=jax.ShapeDtypeStruct((B, B, WIDTH), F32)...  66.2 us
    unnamed x1, local copies, waits for them, and re-layouts  3.16 us

profile of v1, /device:TPU:96, one launch (start us, length us, event | category | flops | bytes accessed | tf_op | source)
XLA Modules:
  0.0 70.0 jit_solution(5301090701133730234)
XLA Ops:
  0.7 66.2 %shard_map.55 = f32[64,64,80]{2,1,0:T(8,128)} custom-call(bf16[8,27,64,64]{3,2,1,0:T(8,128)(2,1)} %blocks_hbm.1, bf16[8,64,64]{2,1,0:T(8,128)(2,1)} %prolong.1, s32[8,27]{1,0:T(8,128)} %ids.1, s32[8,27]{1,0:T(8,128)} %ids.1, s32[8]{0:T(128)} %aggs.1, s32[1]{0:T(128)S(6)} %copy.7.live), custom_call_target="tpu_custom_call" | custom-call | tf_op jit(solution)/shard_map/pallas_call | solution.py:367
  66.8 3.2 %copy.8 = f32[1,80,64,64]{1,3,2,0:T(8,128)} copy(f32[1,80,64,64]{1,3,2,0:T(8,128)} %bitcast.3) | data formatting | bytes 2621440

commit v2 on v1

v2 whole, which is shorter than its diff:
```python
import functools

import jax
import jax.numpy as jnp
from jax import lax
from jax.experimental import pallas as pl
from jax.experimental.pallas import tpu as pltpu
from jax.sharding import PartitionSpec as P

MESH = pl.DeviceIdType.MESH
GRP, SIDE, NCOL = 16, 4, 8
RB, KA, B = 8, 27, 64
KP = 28
CHUNKS, PER = 2, 4
CR = KP * PER
WIDTH = 80
TILES = 160
ORDER = (0, 10, 6, 9, 11, 14, 2, 5, 7, 8, 13, 15, 1, 3, 4, 12)
LAG = 3
BATCH = 4
MSG = 272
HALF = (pl.ds(0, 144), pl.ds(144, 128))
FULL = 32760.0
F32, BF16 = jnp.float32, jnp.bfloat16


def root(x, inverse):
    t = x * inverse
    return t * lax.rsqrt(jnp.maximum(jnp.abs(t), 1e-30))


def short(y):
    return y.astype(jnp.int32).astype(jnp.int16)


def decode(v):
    v = v.astype(F32)
    return v * (jnp.abs(v) + 1.0)


def remote(src, dst, send, recv, where):
    return pltpu.make_async_remote_copy(
        src_ref=src, dst_ref=dst, send_sem=send, recv_sem=recv, device_id=where, device_id_type=MESH
    )


def kernel(
    blocks_hbm, prolong_hbm, ids_hbm, ids, aggs, live,
    got2, scale2,
    prolong, ids_vec, pick, high, lower, blocks, tiles, table, flipped, u, ids_row, stage, out1, got1, keys, total, out2, scale_out,
    tile_sem, ids_sem, block_sem, ag_send, ag_recv, near_send, near_recv,
    d_send, d_recv, e_send, e_recv, f_send, f_recv,
):
    s, g, c = lax.axis_index("slab"), lax.axis_index("grp"), lax.axis_index("col")
    gy, gx = g // SIDE, lax.rem(g, SIDE)
    bar = pltpu.get_barrier_semaphore()
    for p in range(1, GRP):
        pl.semaphore_signal(bar, inc=1, device_id={"grp": lax.rem(g + p, GRP)}, device_id_type=MESH)
    pl.semaphore_signal(bar, inc=1, device_id={"slab": 1 - s}, device_id_type=MESH)

    @pl.when(c > 0)
    def _():
        pl.semaphore_signal(bar, inc=1, device_id={"col": c - 1}, device_id_type=MESH)

    @pl.when(c < NCOL - 1)
    def _():
        pl.semaphore_signal(bar, inc=1, device_id={"col": c + 1}, device_id_type=MESH)

    tile_copy = pltpu.make_async_copy(prolong_hbm, prolong, tile_sem)
    tile_copy.start()

    def block_copy(i):
        return pltpu.make_async_copy(blocks_hbm.at[i], blocks.at[i], block_sem.at[i])

    for i in range(RB):
        block_copy(i).start()
    ids_copy = pltpu.make_async_copy(ids_hbm, ids_vec, ids_sem)
    ids_copy.start()
    tile_copy.wait()

    alive = jnp.full((B, B), live[0], jnp.int32)
    for r in range(0, RB, 2):
        left, right = (
            jnp.where(alive > r + d, prolong[r + d].astype(F32), 0.0) for d in range(2)
        )
        tiles[g, 32 * r : 32 * r + B, :] = jnp.concatenate([left, right], axis=1).astype(BF16)
        flipped[r] = left.T.astype(BF16)
        flipped[r + 1] = right.T.astype(BF16)
    sub16 = lax.broadcasted_iota(jnp.int32, (16, 128), 0)
    agg_rows = jnp.zeros((16, 128), F32)
    for r in range(RB):
        agg_rows = jnp.where(sub16 == r, aggs[r].astype(F32), agg_rows)
    tiles[g, 256:MSG, :] = agg_rows.astype(BF16)

    tiles[GRP + s] = jnp.zeros((MSG, 128), BF16)

    @pl.when(c == 0)
    def _():
        tiles[GRP + 2] = jnp.zeros((MSG, 128), BF16)

    @pl.when(c == NCOL - 1)
    def _():
        tiles[GRP + 3] = jnp.zeros((MSG, 128), BF16)

    def u_row(i, carry):
        block_copy(i).wait()
        for k in range(0, KP, 2):
            left = jnp.dot(flipped[i], blocks[i, k], preferred_element_type=F32)
            if k + 1 < KA:
                right = jnp.dot(flipped[i], blocks[i, k + 1], preferred_element_type=F32)
            else:
                right = jnp.zeros((B, B), F32)
            value = jnp.concatenate([left, right], axis=1)
            high = value.astype(BF16)
            u[i, k // 2, 0:B, :] = high
            u[i, k // 2, B : 2 * B, :] = (value - high.astype(F32)).astype(BF16)
        return carry

    u_row(0, 0)
    cols = (c + NCOL - 1) // NCOL + (2 * NCOL - 2 - c) // NCOL
    pl.semaphore_wait(bar, GRP + cols)

    sends = []

    def spread(slot, half, y, x, source):
        copy = remote(
            tiles.at[slot, HALF[half]],
            tiles.at[slot, HALF[half]],
            ag_send.at[len(sends)],
            ag_recv.at[source * 2 + half],
            {"grp": y * SIDE + x},
        )
        copy.start()
        sends.append(copy)

    def arrived(dy, dx, half):
        slot = lax.rem(gy + dy, SIDE) * SIDE + lax.rem(gx + dx, SIDE)
        remote(
            tiles.at[slot, HALF[half]], tiles.at[slot, HALF[half]],
            ag_send.at[0], ag_recv.at[(dy * SIDE + dx) * 2 + half], {"grp": lax.rem(g + 1, GRP)},
        ).wait_recv()
        return slot

    for d in (1, 3, 2):
        back = SIDE - d
        spread(g, 0, gy, lax.rem(gx + d, SIDE), back)
        spread(g, 1, lax.rem(gy + d, SIDE), gx, back * SIDE)
    for d in (1, 3, 2):
        back = SIDE - d
        spread(g, 1, gy, lax.rem(gx + d, SIDE), back)
        spread(g, 0, lax.rem(gy + d, SIDE), gx, back * SIDE)

    def near(k, slot, where):
        return remote(tiles.at[g], tiles.at[slot], near_send.at[k], near_recv.at[k], where)

    near(0, GRP + s, {"slab": 1 - s}).start()

    @pl.when(c < NCOL - 1)
    def _():
        near(1, GRP + 2, {"col": c + 1}).start()

    @pl.when(c > 0)
    def _():
        near(2, GRP + 3, {"col": c - 1}).start()

    wide = lax.broadcasted_iota(jnp.int32, (B, 128), 1) < B

    def unfold(slot):
        def pair(n, carry):
            both = tiles[slot, pl.ds(pl.multiple_of(n * B, B), B), :].astype(F32)
            turned = pltpu.roll(both, B, 1)
            at = slot * RB + 2 * n
            table[at] = jnp.where(wide, both, 0.0).astype(BF16)
            table[at + 1] = jnp.where(wide, turned, 0.0).astype(BF16)
            table[TILES + at] = jnp.where(wide, 0.0, turned).astype(BF16)
            table[TILES + at + 1] = jnp.where(wide, 0.0, both).astype(BF16)
            return carry

        lax.fori_loop(0, RB // 2, pair, 0)

    for n, e in enumerate((1, 3, 2)):
        lax.fori_loop(1 + n, 2 + n, u_row, 0)
        slot = arrived(0, e, 0)
        for d in (1, 3, 2):
            spread(slot, 0, lax.rem(gy + d, SIDE), gx, (SIDE - d) * SIDE + e)
        slot = arrived(e, 0, 1)
        for d in (1, 3, 2):
            spread(slot, 1, gy, lax.rem(gx + d, SIDE), e * SIDE + SIDE - d)

    lax.fori_loop(4, RB, u_row, 0)
    unfold(g)
    for e in (1, 3, 2):
        unfold(arrived(0, e, 1))
        unfold(arrived(e, 0, 0))
    near(0, GRP + 1 - s, {"slab": 1 - s}).wait_recv()

    @pl.when(c > 0)
    def _():
        near(1, GRP + 2, {"col": c - 1}).wait_recv()

    @pl.when(c < NCOL - 1)
    def _():
        near(2, GRP + 3, {"col": c + 1}).wait_recv()

    for slot in range(GRP, GRP + 4):
        unfold(slot)
    for e in (1, 3, 2):
        for f in (1, 3, 2):
            arrived(e, f, 0)
            unfold(arrived(e, f, 1))

    ids_copy.wait()
    ids_row[...] = jnp.full((8, 128), -1, jnp.int32)
    ids_row[:, 0:KA] = ids_vec[...]
    lane = lax.broadcasted_iota(jnp.int32, (8, 128), 1)
    sub = lax.broadcasted_iota(jnp.int32, (8, 128), 0)
    for ch in range(CHUNKS):
        q = jnp.full((8, 128), -1, jnp.int32)
        owner = jnp.zeros((8, 128), F32)
        for ii in range(PER):
            i = PER * ch + ii
            row = jnp.broadcast_to(ids_row[i : i + 1, :], (8, 128))
            inside = (lane >= KP * ii) & (lane < KP * (ii + 1))
            q = jnp.where(inside, pltpu.roll(row, KP * ii, 1) if ii else row, q)
            owner = jnp.where(inside, aggs[i].astype(F32), owner)
        slot = jnp.zeros((8, 128), F32)
        for d in range(GRP + 4):
            base = 0 if d < GRP else (d - GRP + 1) * GRP
            named = tiles[d, 256:MSG, :].astype(F32)[0:8]
            slot = slot + jnp.where(q == sub + 8 * d, named + base, 0.0)
        slot = jnp.broadcast_to(jnp.sum(slot, axis=0, keepdims=True), (8, 128))
        key = jnp.where(q < 0, -1.0, owner * WIDTH + slot)
        keys[ch] = key

    low = lax.broadcasted_iota(jnp.int32, (8, 128), 1) < B

    def piece(ch, p):
        where = lax.bitwise_xor(g, p)
        return remote(out1.at[ch, where], got1.at[ch, g], d_send.at[ch, p], d_recv.at[ch, p], {"grp": where})

    high[...] = jnp.zeros_like(high)
    lower[...] = jnp.zeros_like(lower)
    pick[...] = jnp.zeros_like(pick)

    def load(ch, n, source):
        v = decode(got1[ch, source])
        top = v.astype(BF16)
        high[n * 128 : n * 128 + CR, :] = top
        lower[n * 128 : n * 128 + CR, :] = (v - top.astype(F32)).astype(BF16)
        key = got1[ch, source, 16:32, 0:128].astype(F32)[KP - 17 : KP - 16, 0:CR]
        unit = jnp.exp2(got1[ch, source, 48:64, 0:128].astype(F32)[2 * KP - 49 : 2 * KP - 48, 0:CR])
        for r in range(0, GRP * WIDTH, 64):
            row = lax.broadcasted_iota(jnp.int32, (64, CR), 0).astype(F32) + float(r)
            pick[r : r + 64, n * 128 : n * 128 + CR] = jnp.where(row == key, unit, 0.0).astype(BF16)

    def batch(ch, first, count):
        for n in range(count):
            p = ORDER[first + n]
            if p:
                piece(ch, p).wait_recv()
            load(ch, n, lax.bitwise_xor(g, p))
        depth = 128 * count
        value = jnp.dot(pick[:, 0:depth], high[0:depth, :], preferred_element_type=F32)
        value = value + jnp.dot(pick[:, 0:depth], lower[0:depth, :], preferred_element_type=F32)
        if ch or first:
            total[...] += value
        else:
            total[...] = value

    row_of = lax.broadcasted_iota(jnp.int32, (CR, 128), 0)
    for ch in range(CHUNKS):
        def t_row(ii, scales, ch=ch):
            i = PER * ch + ii
            top = jnp.zeros((8, 128), F32)
            for k in range(0, KP, 2):
                weights = jnp.concatenate(
                    [table[ids[i, k]], table[TILES + ids[i, min(k + 1, KA - 1)]]], axis=0
                )
                both = jnp.dot(u[i, k // 2], weights, preferred_element_type=F32)
                value = both[0:B] + both[B : 2 * B]
                top = jnp.maximum(top, jnp.max(jnp.abs(value).reshape(8, 8, 128), axis=0))
                for half in range(2):
                    for w in range(2):
                        first = value[32 * w + 8 * half : 32 * w + 8 * half + 8]
                        second = value[32 * w + 16 + 8 * half : 32 * w + 24 + 8 * half]
                        at = CR * (GRP * w + 8 * half) + KP * ii + k
                        stage[pl.ds(at, 8, stride=CR), :] = jnp.where(low, first, pltpu.roll(second, B, 1))
                        stage[pl.ds(at + 1, 8, stride=CR), :] = jnp.where(low, pltpu.roll(first, B, 1), second)
            most = jnp.max(jnp.max(top, axis=1, keepdims=True), axis=0, keepdims=True)
            most = jnp.broadcast_to(most, (8, 128))
            power = jnp.ceil(jnp.log2(jnp.maximum(most, 1e-25) * (1.004 / (FULL * FULL))))
            return tuple(jnp.where(ii == n, power, scales[n]) for n in range(PER))

        scales = lax.fori_loop(0, PER, t_row, tuple(jnp.zeros((8, 128), F32) for _ in range(PER)))
        powers = jnp.zeros((8, 128), F32)
        inverse = jnp.zeros((CR, 128), F32)
        for ii in range(PER):
            powers = jnp.where((lane >= KP * ii) & (lane < KP * (ii + 1)), scales[ii], powers)
            inverse = jnp.where(row_of >= KP * ii, jnp.exp2(-scales[ii])[0:1], inverse)

        def coded(where, ch=ch, inverse=inverse, powers=powers):
            first = root(stage[pl.ds(pl.multiple_of(where * CR, 16), CR), :], inverse)
            second = root(stage[pl.ds(pl.multiple_of((GRP + where) * CR, 16), CR), :], inverse)
            first = jnp.where(row_of == KP - 1, keys[ch][0:1], first)
            first = jnp.where(row_of == 2 * KP - 1, powers[0:1], first)
            return jnp.concatenate([short(first), short(second)], axis=1)

        got1[ch, g] = coded(g)
        for n in range(1, GRP):
            p = ORDER[n]
            where = lax.bitwise_xor(g, p)
            out1[ch, where] = coded(where)
            if ch and n > LAG:
                piece(0, ORDER[n - LAG]).wait_send()
            piece(ch, p).start()
            if ch and n % BATCH == BATCH - 1:
                batch(0, n - BATCH + 1, BATCH)

    batch(1, 0, 4)
    batch(1, 4, 4)
    batch(1, 8, 4)
    batch(1, 12, 2)
    batch(1, 14, 2)

    def home(p):
        where = lax.bitwise_xor(g, p)
        return (
            remote(out2.at[where], got2.at[g], e_send.at[p], e_recv.at[p], {"grp": where}),
            remote(scale_out.at[where], scale2.at[g], f_send.at[p], f_recv.at[p], {"grp": where}),
        )

    def owned(where):
        value = total[pl.ds(pl.multiple_of(where * WIDTH, 16), WIDTH), :]
        most = jnp.max(jnp.max(jnp.abs(value), axis=1, keepdims=True), axis=0, keepdims=True)
        unit = jnp.maximum(most, 1e-25) * (1.004 / (FULL * FULL))
        return short(root(value, 1.0 / unit)), jnp.broadcast_to(unit, (8, 128))

    got2[g], scale2[g] = owned(g)

    for p in ORDER[1:]:
        where = lax.bitwise_xor(g, p)
        out2[where], scale_out[where] = owned(where)
        for copy in home(p):
            copy.start()

    for p in ORDER[1:]:
        for copy in home(p):
            copy.wait()
        piece(1, p).wait_send()
    for p in ORDER[GRP - LAG :]:
        piece(0, p).wait_send()
    for copy in sends:
        copy.wait_send()
    near(0, GRP + s, {"slab": 1 - s}).wait_send()

    @pl.when(c < NCOL - 1)
    def _():
        near(1, GRP + 2, {"col": c + 1}).wait_send()

    @pl.when(c > 0)
    def _():
        near(2, GRP + 3, {"col": c - 1}).wait_send()


def unpack(got, scale, out):
    for m in range(GRP):
        v = decode(got[m]) * scale[m][0:1, 0:1]
        flat = v.T
        for h in range(2):
            out[GRP * h + m] = flat[B * h : B * (h + 1), :]


def per_device(fine_blocks, prolong, column_ids, aggregate_ids, live_rows):
    vmem = pl.BlockSpec(memory_space=pltpu.VMEM)
    hbm = pl.BlockSpec(memory_space=pltpu.HBM)
    smem = pl.BlockSpec(memory_space=pltpu.SMEM)
    dma = pltpu.SemaphoreType.DMA
    coded, scale = pl.pallas_call(
        kernel,
        out_shape=[
            jax.ShapeDtypeStruct((GRP, WIDTH, 256), jnp.int16),
            jax.ShapeDtypeStruct((GRP, 8, 128), F32),
        ],
        in_specs=[hbm, hbm, hbm, smem, smem, smem],
        out_specs=[vmem, vmem],
        scratch_shapes=[
            pltpu.VMEM((RB, B, B), BF16),
            pltpu.VMEM((RB, KA), jnp.int32),
            pltpu.VMEM((GRP * WIDTH, BATCH * 128), BF16),
            pltpu.VMEM((BATCH * 128, 256), BF16),
            pltpu.VMEM((BATCH * 128, 256), BF16),
            pltpu.VMEM((RB, KA, B, B), BF16),
            pltpu.VMEM((GRP + 4, MSG, 128), BF16),
            pltpu.VMEM((2 * TILES, B, 128), BF16),
            pltpu.VMEM((RB, B, B), BF16),
            pltpu.VMEM((RB, KP // 2, 2 * B, 128), BF16),
            pltpu.VMEM((8, 128), jnp.int32),
            pltpu.VMEM((2 * GRP * CR, 128), F32),
            pltpu.VMEM((CHUNKS, GRP, CR, 256), jnp.int16),
            pltpu.VMEM((CHUNKS, GRP, CR, 256), jnp.int16),
            pltpu.VMEM((CHUNKS, 8, 128), F32),
            pltpu.VMEM((GRP * WIDTH, 256), F32),
            pltpu.VMEM((GRP, WIDTH, 256), jnp.int16),
            pltpu.VMEM((GRP, 8, 128), F32),
            dma,
            dma,
            dma((RB,)),
            dma((32,)),
            dma((32,)),
            dma((3,)),
            dma((3,)),
            dma((CHUNKS, GRP)),
            dma((CHUNKS, GRP)),
            dma((GRP,)),
            dma((GRP,)),
            dma((GRP,)),
            dma((GRP,)),
        ],
        compiler_params=pltpu.CompilerParams(
            collective_id=0, has_side_effects=True, vmem_limit_bytes=58 * 2**20
        ),
    )(fine_blocks, prolong, column_ids, column_ids, aggregate_ids, live_rows)
    out = pl.pallas_call(
        unpack,
        grid=(2,),
        out_shape=jax.ShapeDtypeStruct((B, B, WIDTH), F32),
        in_specs=[
            pl.BlockSpec((GRP, WIDTH, 128), lambda j: (0, 0, j)),
            pl.BlockSpec((GRP, 8, 128), lambda j: (0, 0, 0)),
        ],
        out_specs=pl.BlockSpec((2 * GRP, B, WIDTH), lambda j: (j, 0, 0)),
        compiler_params=pltpu.CompilerParams(vmem_limit_bytes=58 * 2**20),
    )(coded, scale)
    return out.transpose(2, 0, 1)[None]


def solution(mesh):
    rows = ("slab", "grp", "col")
    return jax.shard_map(
        per_device,
        mesh=mesh,
        in_specs=(
            P(rows, None, None, None),
            P(rows, None, None),
            P(rows, None),
            P(rows),
            P(rows),
        ),
        out_specs=P(rows, None, None, None),
        check_vma=False,
    )
```

time: 70.1 us -> 61.6 us (0.88)
  Pallas kernels: 66.2 us -> 60.4 us
  local copies, waits for them, and re-layouts: 3.16 us -> 0 us
    pallas_call x1 -> x2, Pallas kernels: 66.2 us -> 60.4 us  [the longest x1 57.6 us: per_device(): pl.pallas_call(kernel, out_shape=[jax.ShapeDtypeStruct((GRP, WIDTH, 256),...]
    unnamed x1 -> x0, local copies, waits for them, and re-layouts: 3.16 us -> none
where the time goes in v2:
time: 61.6 us; the launch traced here: 61.1 us
  Pallas kernels  60.4 us (98%)
  between operations  0.66 us (1%)
    pallas_call x1, Pallas kernels, per_device(): pl.pallas_call(kernel, out_shape=[jax.ShapeDtypeStruct((GRP, WIDTH, 256),...  57.6 us
    pallas_call x1, Pallas kernels, per_device(): pl.pallas_call(unpack, grid=(2,), out_shape=jax.ShapeDtypeStruct((B, B, W...  2.77 us

profile of v2, /device:TPU:96, one launch (start us, length us, event | category | flops | bytes accessed | tf_op | source)
XLA Modules:
  0.0 61.1 jit_solution(16719932738505958010)
XLA Ops:
  0.7 57.6 %shard_map.55 = (s16[16,80,256]{2,1,0:T(8,128)(2,1)}, f32[16,8,128]{2,1,0:T(8,128)}) custom-call(bf16[8,27,64,64]{3,2,1,0:T(8,128)(2,1)} %blocks_hbm.1, bf16[8,64,64]{2,1,0:T(8,128)(2,1)} %prolong_hbm.1, s32[8,27]{1,0:T(8,128)} %ids.1, s32[8,27]{1,0:T(8,128)} %ids.1, s32[8]{0:T(128)} %aggs.1, s32[1]{0:T(128)S(6)} %copy.6.live), custom_call_target="tpu_custom_call" | custom-call | tf_op jit(solution)/shard_map/pallas_call | solution.py:378
  58.3 2.8 %shard_map.56 = f32[64,64,80]{2,1,0:T(8,128)} custom-call(s16[16,80,256]{2,1,0:T(8,128)(2,1)} %get-tuple-element.7.got, f32[16,8,128]{2,1,0:T(8,128)} %get-tuple-element.8.scale), custom_call_target="tpu_custom_call" | custom-call | tf_op jit(solution)/shard_map/pallas_call | solution.py:423

commit v3 on v2

--- a/solution.py
+++ b/solution.py
@@ -15,6 +15,7 @@
 CR = KP * PER
 WIDTH = 80
 TILES = 160
+EARLY = 2
 ORDER = (0, 10, 6, 9, 11, 14, 2, 5, 7, 8, 13, 15, 1, 3, 4, 12)
 LAG = 3
 BATCH = 4
@@ -45,10 +46,10 @@
 
 
 def kernel(
-    blocks_hbm, prolong_hbm, ids_hbm, ids, aggs, live,
+    blocks_hbm, prolong_hbm, ids_hbm, aggs_hbm, live_hbm,
     got2, scale2,
-    prolong, ids_vec, pick, high, lower, blocks, tiles, table, flipped, u, ids_row, stage, out1, got1, keys, total, out2, scale_out,
-    tile_sem, ids_sem, block_sem, ag_send, ag_recv, near_send, near_recv,
+    prolong, ids_vec, ids, aggs, live, pick, high, lower, blocks, tiles, table, flipped, u, ids_row, stage, out1, got1, keys, total, out2, scale_out,
+    small_sem, block_sem, ag_send, ag_recv, near_send, near_recv,
     d_send, d_recv, e_send, e_recv, f_send, f_recv,
 ):
     s, g, c = lax.axis_index("slab"), lax.axis_index("grp"), lax.axis_index("col")
@@ -66,17 +67,22 @@
     def _():
         pl.semaphore_signal(bar, inc=1, device_id={"col": c + 1}, device_id_type=MESH)
 
-    tile_copy = pltpu.make_async_copy(prolong_hbm, prolong, tile_sem)
-    tile_copy.start()
+    small = [
+        pltpu.make_async_copy(src, dst, small_sem.at[n])
+        for n, (src, dst) in enumerate(
+            ((prolong_hbm, prolong), (live_hbm, live), (aggs_hbm, aggs), (ids_hbm, ids_vec), (ids_hbm, ids))
+        )
+    ]
+    for copy in small:
+        copy.start()
 
     def block_copy(i):
         return pltpu.make_async_copy(blocks_hbm.at[i], blocks.at[i], block_sem.at[i])
 
     for i in range(RB):
         block_copy(i).start()
-    ids_copy = pltpu.make_async_copy(ids_hbm, ids_vec, ids_sem)
-    ids_copy.start()
-    tile_copy.wait()
+    for copy in small[:3]:
+        copy.wait()
 
     alive = jnp.full((B, B), live[0], jnp.int32)
     for r in range(0, RB, 2):
@@ -116,7 +122,7 @@
             u[i, k // 2, B : 2 * B, :] = (value - high.astype(F32)).astype(BF16)
         return carry
 
-    u_row(0, 0)
+    lax.fori_loop(0, EARLY, u_row, 0)
     cols = (c + NCOL - 1) // NCOL + (2 * NCOL - 2 - c) // NCOL
     pl.semaphore_wait(bar, GRP + cols)
 
@@ -164,22 +170,24 @@
         near(2, GRP + 3, {"col": c - 1}).start()
 
     wide = lax.broadcasted_iota(jnp.int32, (B, 128), 1) < B
+    first_half = jnp.where(wide, 1.0, 0.0).astype(BF16)
+    second_half = jnp.where(wide, 0.0, 1.0).astype(BF16)
 
     def unfold(slot):
         def pair(n, carry):
-            both = tiles[slot, pl.ds(pl.multiple_of(n * B, B), B), :].astype(F32)
-            turned = pltpu.roll(both, B, 1)
+            both = tiles[slot, pl.ds(pl.multiple_of(n * B, B), B), :]
+            turned = pltpu.roll(both.astype(F32), B, 1).astype(BF16)
             at = slot * RB + 2 * n
-            table[at] = jnp.where(wide, both, 0.0).astype(BF16)
-            table[at + 1] = jnp.where(wide, turned, 0.0).astype(BF16)
-            table[TILES + at] = jnp.where(wide, 0.0, turned).astype(BF16)
-            table[TILES + at + 1] = jnp.where(wide, 0.0, both).astype(BF16)
+            table[at] = both * first_half
+            table[at + 1] = turned * first_half
+            table[TILES + at] = turned * second_half
+            table[TILES + at + 1] = both * second_half
             return carry
 
         lax.fori_loop(0, RB // 2, pair, 0)
 
     for n, e in enumerate((1, 3, 2)):
-        lax.fori_loop(1 + n, 2 + n, u_row, 0)
+        lax.fori_loop(EARLY + n, EARLY + n + 1, u_row, 0)
         slot = arrived(0, e, 0)
         for d in (1, 3, 2):
             spread(slot, 0, lax.rem(gy + d, SIDE), gx, (SIDE - d) * SIDE + e)
@@ -187,7 +195,7 @@
         for d in (1, 3, 2):
             spread(slot, 1, gy, lax.rem(gx + d, SIDE), e * SIDE + SIDE - d)
 
-    lax.fori_loop(4, RB, u_row, 0)
+    lax.fori_loop(EARLY + 3, RB, u_row, 0)
     unfold(g)
     for e in (1, 3, 2):
         unfold(arrived(0, e, 1))
@@ -209,7 +217,8 @@
             arrived(e, f, 0)
             unfold(arrived(e, f, 1))
 
-    ids_copy.wait()
+    for copy in small[3:]:
+        copy.wait()
     ids_row[...] = jnp.full((8, 128), -1, jnp.int32)
     ids_row[:, 0:KA] = ids_vec[...]
     lane = lax.broadcasted_iota(jnp.int32, (8, 128), 1)
@@ -373,7 +382,6 @@
 def per_device(fine_blocks, prolong, column_ids, aggregate_ids, live_rows):
     vmem = pl.BlockSpec(memory_space=pltpu.VMEM)
     hbm = pl.BlockSpec(memory_space=pltpu.HBM)
-    smem = pl.BlockSpec(memory_space=pltpu.SMEM)
     dma = pltpu.SemaphoreType.DMA
     coded, scale = pl.pallas_call(
         kernel,
@@ -381,11 +389,14 @@
             jax.ShapeDtypeStruct((GRP, WIDTH, 256), jnp.int16),
             jax.ShapeDtypeStruct((GRP, 8, 128), F32),
         ],
-        in_specs=[hbm, hbm, hbm, smem, smem, smem],
+        in_specs=[hbm] * 5,
         out_specs=[vmem, vmem],
         scratch_shapes=[
             pltpu.VMEM((RB, B, B), BF16),
             pltpu.VMEM((RB, KA), jnp.int32),
+            pltpu.SMEM((RB, KA), jnp.int32),
+            pltpu.SMEM((RB,), jnp.int32),
+            pltpu.SMEM((1,), jnp.int32),
             pltpu.VMEM((GRP * WIDTH, BATCH * 128), BF16),
             pltpu.VMEM((BATCH * 128, 256), BF16),
             pltpu.VMEM((BATCH * 128, 256), BF16),
@@ -402,8 +413,7 @@
             pltpu.VMEM((GRP * WIDTH, 256), F32),
             pltpu.VMEM((GRP, WIDTH, 256), jnp.int16),
             pltpu.VMEM((GRP, 8, 128), F32),
-            dma,
-            dma,
+            dma((5,)),
             dma((RB,)),
             dma((32,)),
             dma((32,)),
@@ -419,7 +429,7 @@
         compiler_params=pltpu.CompilerParams(
             collective_id=0, has_side_effects=True, vmem_limit_bytes=58 * 2**20
         ),
-    )(fine_blocks, prolong, column_ids, column_ids, aggregate_ids, live_rows)
+    )(fine_blocks, prolong, column_ids, aggregate_ids, live_rows)
     out = pl.pallas_call(
         unpack,
         grid=(2,),

time: 61.6 us -> 60.5 us (0.982)
  Pallas kernels: 60.4 us -> 59.7 us
    pallas_call x1, Pallas kernels: 57.6 us -> 56.9 us  [per_device(): pl.pallas_call(kernel, out_shape=[jax.ShapeDtypeStruct((GRP, WIDTH, 256),...]
where the time goes in v3:
time: 60.5 us; the launch traced here: 60.4 us
  Pallas kernels  59.7 us (99%)
  between operations  0.66 us (1%)
    pallas_call x1, Pallas kernels, per_device(): pl.pallas_call(kernel, out_shape=[jax.ShapeDtypeStruct((GRP, WIDTH, 256),...  56.9 us
    pallas_call x1, Pallas kernels, per_device(): pl.pallas_call(unpack, grid=(2,), out_shape=jax.ShapeDtypeStruct((B, B, W...  2.77 us

profile of v3, /device:TPU:96, one launch (start us, length us, event | category | flops | bytes accessed | tf_op | source)
XLA Modules:
  0.0 60.4 jit_solution(12995225312958588585)
XLA Ops:
  0.7 56.9 %shard_map.55 = (s16[16,80,256]{2,1,0:T(8,128)(2,1)}, f32[16,8,128]{2,1,0:T(8,128)}) custom-call(bf16[8,27,64,64]{3,2,1,0:T(8,128)(2,1)} %blocks_hbm.1, bf16[8,64,64]{2,1,0:T(8,128)(2,1)} %prolong_hbm.1, s32[8,27]{1,0:T(8,128)} %ids_hbm.1, s32[8]{0:T(128)} %aggs_hbm.1, s32[1]{0:T(128)S(6)} %copy.6.live_hbm), custom_call_target="tpu_custom_call" | custom-call | tf_op jit(solution)/shard_map/pallas_call | solution.py:386
  57.6 2.8 %shard_map.56 = f32[64,64,80]{2,1,0:T(8,128)} custom-call(s16[16,80,256]{2,1,0:T(8,128)(2,1)} %get-tuple-element.7.got, f32[16,8,128]{2,1,0:T(8,128)} %get-tuple-element.8.scale), custom_call_target="tpu_custom_call" | custom-call | tf_op jit(solution)/shard_map/pallas_call | solution.py:433

commit v4 on v3

--- a/solution.py
+++ b/solution.py
@@ -15,7 +15,7 @@
 CR = KP * PER
 WIDTH = 80
 TILES = 160
-EARLY = 2
+EARLY = 4
 ORDER = (0, 10, 6, 9, 11, 14, 2, 5, 7, 8, 13, 15, 1, 3, 4, 12)
 LAG = 3
 BATCH = 4
@@ -342,7 +342,7 @@
         value = total[pl.ds(pl.multiple_of(where * WIDTH, 16), WIDTH), :]
         most = jnp.max(jnp.max(jnp.abs(value), axis=1, keepdims=True), axis=0, keepdims=True)
         unit = jnp.maximum(most, 1e-25) * (1.004 / (FULL * FULL))
-        return short(root(value, 1.0 / unit)), jnp.broadcast_to(unit, (8, 128))
+        return short(root(value, 1.0 / unit)), jnp.broadcast_to(unit, (1, 128))
 
     got2[g], scale2[g] = owned(g)
 
@@ -387,7 +387,7 @@
         kernel,
         out_shape=[
             jax.ShapeDtypeStruct((GRP, WIDTH, 256), jnp.int16),
-            jax.ShapeDtypeStruct((GRP, 8, 128), F32),
+            jax.ShapeDtypeStruct((GRP, 1, 128), F32),
         ],
         in_specs=[hbm] * 5,
         out_specs=[vmem, vmem],
@@ -412,7 +412,7 @@
             pltpu.VMEM((CHUNKS, 8, 128), F32),
             pltpu.VMEM((GRP * WIDTH, 256), F32),
             pltpu.VMEM((GRP, WIDTH, 256), jnp.int16),
-            pltpu.VMEM((GRP, 8, 128), F32),
+            pltpu.VMEM((GRP, 1, 128), F32),
             dma((5,)),
             dma((RB,)),
             dma((32,)),
@@ -436,7 +436,7 @@
         out_shape=jax.ShapeDtypeStruct((B, B, WIDTH), F32),
         in_specs=[
             pl.BlockSpec((GRP, WIDTH, 128), lambda j: (0, 0, j)),
-            pl.BlockSpec((GRP, 8, 128), lambda j: (0, 0, 0)),
+            pl.BlockSpec((GRP, 1, 128), lambda j: (0, 0, 0)),
         ],
         out_specs=pl.BlockSpec((2 * GRP, B, WIDTH), lambda j: (j, 0, 0)),
         compiler_params=pltpu.CompilerParams(vmem_limit_bytes=58 * 2**20),

time: 60.5 us -> 59.5 us (0.983)
  Pallas kernels: 59.7 us -> 58.7 us
    pallas_call x1, Pallas kernels: 56.9 us -> 55.9 us  [per_device(): pl.pallas_call(kernel, out_shape=[jax.ShapeDtypeStruct((GRP, WIDTH, 256),...]
where the time goes in v4:
time: 59.5 us; the launch traced here: 59.4 us
  Pallas kernels  58.7 us (99%)
  between operations  0.66 us (1%)
    pallas_call x1, Pallas kernels, per_device(): pl.pallas_call(kernel, out_shape=[jax.ShapeDtypeStruct((GRP, WIDTH, 256),...  55.9 us
    pallas_call x1, Pallas kernels, per_device(): pl.pallas_call(unpack, grid=(2,), out_shape=jax.ShapeDtypeStruct((B, B, W...  2.79 us

profile of v4, /device:TPU:96, one launch (start us, length us, event | category | flops | bytes accessed | tf_op | source)
XLA Modules:
  0.0 59.4 jit_solution(6884920011966363041)
XLA Ops:
  0.7 55.9 %shard_map.55 = (s16[16,80,256]{2,1,0:T(8,128)(2,1)}, f32[16,1,128]{2,1,0:T(1,128)}) custom-call(bf16[8,27,64,64]{3,2,1,0:T(8,128)(2,1)} %blocks_hbm.1, bf16[8,64,64]{2,1,0:T(8,128)(2,1)} %prolong_hbm.1, s32[8,27]{1,0:T(8,128)} %ids_hbm.1, s32[8]{0:T(128)} %aggs_hbm.1, s32[1]{0:T(128)S(6)} %copy.6.live_hbm), custom_call_target="tpu_custom_call" | custom-call | tf_op jit(solution)/shard_map/pallas_call | solution.py:386
  56.6 2.8 %shard_map.56 = f32[64,64,80]{2,1,0:T(8,128)} custom-call(s16[16,80,256]{2,1,0:T(8,128)(2,1)} %get-tuple-element.7.got, f32[16,1,128]{2,1,0:T(1,128)} %get-tuple-element.8.scale), custom_call_target="tpu_custom_call" | custom-call | tf_op jit(solution)/shard_map/pallas_call | solution.py:433

commit v5 on v4

--- a/solution.py
+++ b/solution.py
@@ -15,7 +15,7 @@
 CR = KP * PER
 WIDTH = 80
 TILES = 160
-EARLY = 4
+EARLY = 5
 ORDER = (0, 10, 6, 9, 11, 14, 2, 5, 7, 8, 13, 15, 1, 3, 4, 12)
 LAG = 3
 BATCH = 4

time: 59.5 us -> 59.1 us (level)
  no operation moved by 1% of the time
where the time goes in v5:
time: 59.1 us; the launch traced here: 59 us
  Pallas kernels  58.3 us (99%)
  between operations  0.66 us (1%)
    pallas_call x1, Pallas kernels, per_device(): pl.pallas_call(kernel, out_shape=[jax.ShapeDtypeStruct((GRP, WIDTH, 256),...  55.6 us
    pallas_call x1, Pallas kernels, per_device(): pl.pallas_call(unpack, grid=(2,), out_shape=jax.ShapeDtypeStruct((B, B, W...  2.79 us

profile of v5, /device:TPU:96, one launch (start us, length us, event | category | flops | bytes accessed | tf_op | source)
XLA Modules:
  0.0 59.0 jit_solution(15792312940862707163)
XLA Ops:
  0.7 55.6 %shard_map.55 = (s16[16,80,256]{2,1,0:T(8,128)(2,1)}, f32[16,1,128]{2,1,0:T(1,128)}) custom-call(bf16[8,27,64,64]{3,2,1,0:T(8,128)(2,1)} %blocks_hbm.1, bf16[8,64,64]{2,1,0:T(8,128)(2,1)} %prolong_hbm.1, s32[8,27]{1,0:T(8,128)} %ids_hbm.1, s32[8]{0:T(128)} %aggs_hbm.1, s32[1]{0:T(128)S(6)} %copy.6.live_hbm), custom_call_target="tpu_custom_call" | custom-call | tf_op jit(solution)/shard_map/pallas_call | solution.py:386
  56.2 2.8 %shard_map.56 = f32[64,64,80]{2,1,0:T(8,128)} custom-call(s16[16,80,256]{2,1,0:T(8,128)(2,1)} %get-tuple-element.7.got, f32[16,1,128]{2,1,0:T(1,128)} %get-tuple-element.8.scale), custom_call_target="tpu_custom_call" | custom-call | tf_op jit(solution)/shard_map/pallas_call | solution.py:433
